TPU v7x, 32 devices: a whole 2x2x4 slice. The times are simulated.
32 devices in a mesh: groups: 2 (over y), tile: 4 (over z), face: 4 (over x, core).
Axes of the slice: x: 2, y: 2, z: 4, core: 2. Of those that a mesh axis runs over, the one named last changes fastest.
Arguments:
- noisy_state: float32 [24, 256, 512], P('groups', 'face', 'tile'), parts along dimension 0, may hold values from -6 to 6
- conditioning: float32 [24, 256, 512], P('groups', 'face', 'tile'), parts along dimension 0, may hold values from -6 to 6
- orient: int32 [4, 8], replicated, may hold values from 0 to 3
- corner_points: int32 [4, 8], replicated, may hold values 0 or 1
- w_state: bfloat16 [128, 108], replicated, may hold values from -0.625 to 0.625
- w_cond: bfloat16 [128, 108], replicated, may hold values from -0.625 to 0.625
- w_out: bfloat16 [108, 128], replicated, may hold values from -0.1875 to 0.1875
- embed_first: float32 [128], replicated, may hold values from -3 to 3
- embed_second: float32 [128], replicated, may hold values from -3 to 3
Outputs:
- next_state: float32 [24, 256, 512], P('groups', 'face', 'tile'), parts along dimension 0
There are 2 independent parts, one for each index of `groups`. A program takes and returns all parts, laid end to end along the dimension named above; an argument that names none is the same for every part. Nothing has to cross between parts.
Inputs may be any that keep to these rules, and one draw needn't show every extreme that they name: `orient`: A tile's stored pixels are its pixels in the grid's frame turned by this many quarter turns. `corner_points`: entry (r, c) belongs to the upper-left corner of tile (r, c).
All inputs are finite; a program needn't handle non-finite values.
Results may differ from a plain program's by a relative error of at most 0.0019.
Values sent between devices are 32-bit elements; how exact they have to be, the bound alone decides.
A program may use at most 256 MiB of HBM per device.

v0:
```python
import functools
import math

import jax
import jax.numpy as jnp
from jax import lax
from jax.experimental import pallas as pl
from jax.experimental.pallas import tpu as pltpu
from jax.sharding import PartitionSpec as P

RIM = 8
PAD = 16
MESH = pl.DeviceIdType.MESH

guide_weight = 2.0
sigma_first = 1.0
sigma_second = 0.6
step_size = sigma_second - sigma_first
scale_first = 1.0 / math.sqrt(1.0 + sigma_first**2)
scale_second = 1.0 / math.sqrt(1.0 + sigma_second**2)


def corner_flags(corner_points, tile_row, tile_col):
    grid_rows, grid_cols = corner_points.shape
    next_row = (tile_row + 1) % grid_rows
    next_col = (tile_col + 1) % grid_cols
    return (
        corner_points[tile_row, tile_col],
        corner_points[tile_row, next_col],
        corner_points[next_row, tile_col],
        corner_points[next_row, next_col],
    )


def turned(picture, code):
    picture = jnp.where(code % 2 == 1, jnp.swapaxes(picture, -1, -2), picture)
    picture = jnp.where((code == 1) | (code == 2), picture[..., ::-1, :], picture)
    return jnp.where(code >= 2, picture[..., ::-1], picture)


def lane_masks(corner_cuts, side, width):
    lane = jnp.arange(width, dtype=jnp.int32)
    masks = []
    for position, cut in enumerate(corner_cuts):
        col = (lane - (position * side - RIM)) % width
        valid = col < side + 2 * RIM
        left = col < RIM
        right = valid & (col >= side + RIM)
        top = valid & ~(left & (cut[0] == 1)) & ~(right & (cut[1] == 1))
        low = valid & ~(left & (cut[2] == 1)) & ~(right & (cut[3] == 1))
        masks.append(jnp.stack([top, valid, low]))
    return jnp.broadcast_to(
        jnp.stack(masks).astype(jnp.float32)[:, :, None, :], (len(corner_cuts), 3, PAD, width)
    )


def inverse_coverage(corner_cuts, side):
    local_col = jnp.arange(side, dtype=jnp.int32)
    left = local_col < RIM
    right = local_col >= side - RIM
    rows = []
    for kind in range(3):
        parts = []
        for cut in corner_cuts:
            cover = 1.0 + left.astype(jnp.float32) + right.astype(jnp.float32)
            if kind != 1:
                first, second = (cut[0], cut[1]) if kind == 0 else (cut[2], cut[3])
                cover = cover + 1.0
                cover = cover + (left & (first == 0)).astype(jnp.float32)
                cover = cover + (right & (second == 0)).astype(jnp.float32)
            parts.append(cover)
        rows.append(jnp.concatenate(parts))
    cover = jnp.stack(rows)
    return jnp.broadcast_to((1.0 / cover)[:, None, :], (3, PAD, cover.shape[1]))


def tap_variants(taps):
    return jnp.stack([jnp.rot90(taps, (4 - quarter) % 4, axes=(0, 1)) for quarter in range(4)])


def kernel(
    side,
    gs, gc, wm, wc, wo, e1, e2, msk, icov,
    out,
    exs, exc, exm, win, feat, prod, total, sl1,
    ps, pr, fr, fps, fpr,
    send, recv,
):
    width = gs.shape[2]
    extent = side + 2 * RIM
    blocks = extent // RIM
    tiles = wm.shape[0]
    n_tile = lax.axis_size("tile")
    n_face = lax.axis_size("face")
    my_tile = lax.axis_index("tile")
    my_face = lax.axis_index("face")

    def device(d_tile, d_face):
        return {
            "tile": lax.rem(my_tile + d_tile + n_tile, n_tile),
            "face": lax.rem(my_face + d_face + n_face, n_face),
        }

    around = [(dt, df) for dt in (-1, 0, 1) for df in (-1, 0, 1) if (dt, df) != (0, 0)]
    barrier = pltpu.get_barrier_semaphore()
    for dt, df in around:
        pl.semaphore_signal(barrier, inc=1, device_id=device(dt, df), device_id_type=MESH)
    pl.semaphore_wait(barrier, len(around))

    lane = lax.broadcasted_iota(jnp.int32, (PAD, width), 1)
    slots = (blocks + 2) // 2

    def remote(src, dst, phase, number, dt, df):
        return pltpu.make_async_remote_copy(
            src_ref=src,
            dst_ref=dst,
            send_sem=send.at[phase, number],
            recv_sem=recv.at[phase, number],
            device_id=device(dt, df),
            device_id_type=MESH,
        )

    def packed(load, shift, first):
        value = jnp.zeros((PAD, width), jnp.float32)
        for k in range(RIM):
            place = k + first
            moved = pltpu.roll(load(k), lax.rem(shift + RIM * place, width), 1)
            value = jnp.where(lane // RIM == place, moved, value)
        return value

    def unpacked(slot, shift, place):
        return pltpu.roll(slot, lax.rem(2 * width - shift - RIM * place, width), 1)

    def kind_of(block, low, high):
        return jnp.where(block == low, 0, jnp.where(block == high, 2, 1))

    def start_exchange(ex, phase, buf):
        def pack_block(block, _):
            slot = (block + 1) // 2
            first = RIM * lax.rem(block + 1, 2)
            for group in range(2):
                part = packed(lambda k: ex[block * RIM + k], RIM * group, first)
                ps[buf, group, slot] = ps[buf, group, slot] + part
            return 0

        ps[buf] = jnp.zeros(ps.shape[1:], jnp.float32)
        lax.fori_loop(1, blocks - 1, pack_block, 0)
        copies = [
            remote(ex.at[pl.ds(RIM, RIM)], ex.at[pl.ds(side + RIM, RIM)], phase, 0, 0, -1),
            remote(ex.at[pl.ds(side, RIM)], ex.at[pl.ds(0, RIM)], phase, 1, 0, 1),
        ]
        for group, dt in ((0, -1), (1, 1)):
            base = 2 + 3 * group
            mid = pl.ds(1, slots - 2)
            copies += [
                remote(ps.at[buf, group, mid], pr.at[buf, group, mid], phase, base, dt, 0),
                remote(
                    ps.at[buf, group, 1], pr.at[buf, group, slots - 1], phase, base + 1, dt, -1
                ),
                remote(
                    ps.at[buf, group, slots - 2], pr.at[buf, group, 0], phase, base + 2, dt, 1
                ),
            ]
        for copy in copies:
            copy.start()
        return copies

    def finish(copies):
        for copy in copies:
            copy.wait()

    def windows(ex, buf, scale):
        for p in range(tiles):
            for b in range(3):
                win[p, b, 0] = jnp.zeros((PAD, width), jnp.bfloat16)
                win[p, b, extent + 1] = jnp.zeros((PAD, width), jnp.bfloat16)

        def window_block(block, _):
            kind = kind_of(block, 0, blocks - 1)
            slot = (block + 1) // 2
            first = RIM * lax.rem(block + 1, 2)
            after = pr[buf, 0, slot]
            before = pr[buf, 1, slot]
            for k in range(RIM):
                row = block * RIM + k
                body = ex[row]
                left = jnp.where(lane >= width - RIM, unpacked(before, RIM, first + k), body)
                right = jnp.where(lane < RIM, unpacked(after, 0, first + k), body)
                for p, picture in ((0, left), (1, right)):
                    value = jnp.where(msk[p, kind] > 0, scale * picture, 0.0)
                    win[p, 0, row + 1] = pltpu.roll(value, 1, 1).astype(jnp.bfloat16)
                    win[p, 1, row + 1] = value.astype(jnp.bfloat16)
                    win[p, 2, row + 1] = pltpu.roll(value, width - 1, 1).astype(jnp.bfloat16)
            return 0

        lax.fori_loop(0, blocks, window_block, 0)

    def patch(p, first_row):
        taps = []
        for a in range(3):
            for b in range(3):
                rows = win[p, b, pl.ds(first_row + a, RIM)]
                taps.append(jnp.concatenate([rows[r] for r in range(RIM)], axis=1))
        return jnp.concatenate(taps, axis=0)

    def features():
        def feature_block(step, _):
            p = step // blocks
            block = lax.rem(step, blocks)
            feat[p, block] = jnp.dot(
                wc[p], patch(p, block * RIM), preferred_element_type=jnp.float32
            )
            return 0

        lax.fori_loop(0, tiles * blocks, feature_block, 0)

    def predictions(embedding):
        def predict_block(step, _):
            p = step // blocks
            block = lax.rem(step, blocks)
            mixed = jnp.dot(wm[p], patch(p, block * RIM), preferred_element_type=jnp.float32)
            mixed = mixed + embedding[...]
            cond = mixed + feat[p, block]
            plain_hidden = (mixed + mixed * jnp.tanh(mixed)).astype(jnp.bfloat16)
            cond_hidden = (cond + cond * jnp.tanh(cond)).astype(jnp.bfloat16)
            both = jnp.concatenate([cond_hidden, plain_hidden], axis=0)
            z = jnp.dot(wo[p], both, preferred_element_type=jnp.float32)
            for r in range(RIM):
                prod[p, block * RIM + 1 + r] = z[:, r * width : (r + 1) * width]
            return 0

        lax.fori_loop(0, tiles * blocks, predict_block, 0)

    def start_fold(phase, buf):
        fps[buf] = jnp.zeros(fps.shape[1:], jnp.float32)

        def spread_block(block, _):
            kind = kind_of(block, 0, blocks - 1)
            slot = (block + 1) // 2
            first = RIM * lax.rem(block + 1, 2)
            halves = ([], [])
            for k in range(RIM):
                row = block * RIM + k
                outs = []
                for p in range(tiles):
                    acc = []
                    for b in range(3):
                        acc.append(
                            prod[p, row, pl.ds(PAD * b, PAD)]
                            + prod[p, row + 1, pl.ds(PAD * (3 + b), PAD)]
                            + prod[p, row + 2, pl.ds(PAD * (6 + b), PAD)]
                        )
                    valid = msk[p, 1]
                    summed = (
                        acc[1]
                        + pltpu.roll(acc[0] * valid, 1, 1)
                        + pltpu.roll(acc[2] * valid, width - 1, 1)
                    )
                    outs.append(summed * msk[p, kind])
                total[buf, row] = jnp.where(lane < 3 * width // 4, outs[0], 0.0) + jnp.where(
                    lane >= width // 4, outs[1], 0.0
                )
                halves[0].append(outs[1])
                halves[1].append(outs[0])
            for group in range(2):
                part = packed(lambda k: halves[group][k], RIM * group, first)
                fps[buf, group, slot] = fps[buf, group, slot] + part
            return 0

        lax.fori_loop(0, blocks, spread_block, 0)
        copies = [
            remote(total.at[buf, pl.ds(0, RIM)], fr.at[buf, 1], phase, 0, 0, -1),
            remote(total.at[buf, pl.ds(side + RIM, RIM)], fr.at[buf, 0], phase, 1, 0, 1),
        ]
        for group, dt in ((0, 1), (1, -1)):
            base = 2 + 3 * group
            mid = pl.ds(1, slots - 2)
            copies += [
                remote(fps.at[buf, group, mid], fpr.at[buf, group, mid], phase, base, dt, 0),
                remote(fps.at[buf, group, 0], fpr.at[buf, group, 0], phase, base + 1, dt, -1),
                remote(
                    fps.at[buf, group, slots - 1],
                    fpr.at[buf, group, slots - 1],
                    phase,
                    base + 2,
                    dt,
                    1,
                ),
            ]
        for copy in copies:
            copy.start()
        return copies

    def fold(buf, use):
        for group in range(2):
            fpr[buf, group, slots - 2] = fpr[buf, group, slots - 2] + fpr[buf, group, 0]
            fpr[buf, group, 1] = fpr[buf, group, 1] + fpr[buf, group, slots - 1]
        total[buf, pl.ds(RIM, RIM)] = total[buf, pl.ds(RIM, RIM)] + fr[buf, 0]
        total[buf, pl.ds(side, RIM)] = total[buf, pl.ds(side, RIM)] + fr[buf, 1]

        def fold_block(block, _):
            kind = kind_of(block, 1, blocks - 2)
            slot = (block + 1) // 2
            first = RIM * lax.rem(block + 1, 2)
            low = fpr[buf, 0, slot]
            high = fpr[buf, 1, slot]
            scale = icov[kind]
            for k in range(RIM):
                row = block * RIM + k
                value = total[buf, row]
                value = value + jnp.where(lane < RIM, unpacked(low, 0, first + k), 0.0)
                value = value + jnp.where(
                    lane >= width - RIM, unpacked(high, RIM, first + k), 0.0
                )
                use(row, value * scale)
            return 0

        lax.fori_loop(1, blocks - 1, fold_block, 0)

    exc[pl.ds(RIM, side)] = gc[...]
    cond_copies = start_exchange(exc, 0, 0)
    exs[pl.ds(RIM, side)] = gs[...]
    state_copies = start_exchange(exs, 1, 1)
    for p in range(tiles):
        prod[p, 0] = jnp.zeros(prod.shape[2:], jnp.float32)
        prod[p, extent + 1] = jnp.zeros(prod.shape[2:], jnp.float32)
    finish(cond_copies)
    windows(exc, 0, 1.0)
    features()
    finish(state_copies)
    windows(exs, 1, scale_first)
    predictions(e1)
    copies = start_fold(2, 0)
    finish(copies)

    def first_use(row, slope):
        sl1[row - RIM] = slope
        exm[row] = gs[row - RIM] + step_size * slope

    fold(0, first_use)
    copies = start_exchange(exm, 3, 2)
    finish(copies)
    windows(exm, 2, scale_second)
    predictions(e2)
    copies = start_fold(4, 1)
    finish(copies)

    def second_use(row, slope):
        out[row - RIM] = gs[row - RIM] + 0.5 * step_size * (sl1[row - RIM] + slope)

    fold(1, second_use)


def local(
    noisy_state,
    conditioning,
    orient,
    corner_points,
    w_state,
    w_cond,
    w_out,
    embed_first,
    embed_second,
):
    fields, side, width = noisy_state.shape
    tiles = width // side
    extent = side + 2 * RIM
    hidden = w_state.shape[0]
    tile_row = lax.axis_index("face")
    col_base = lax.axis_index("tile") * tiles
    codes = lax.dynamic_slice(orient, (tile_row, col_base), (1, tiles))[0]

    def into_rows(field):
        parts = [
            turned(field[:, :, p * side : (p + 1) * side], (4 - codes[p]) % 4)
            for p in range(tiles)
        ]
        whole = jnp.transpose(jnp.concatenate(parts, axis=2), (1, 0, 2))
        return jnp.pad(whole, ((0, 0), (0, PAD - fields), (0, 0)))

    gs = into_rows(noisy_state)
    gc = into_rows(conditioning)

    def inner_weights(weights):
        taps = weights.reshape(hidden, 3, 3, fields).transpose(1, 2, 0, 3)
        variants = jnp.pad(tap_variants(taps), ((0, 0),) * 4 + ((0, PAD - fields),))
        variants = variants.transpose(0, 3, 1, 2, 4).reshape(4, hidden, 9 * PAD)
        return (0.5 * variants[codes]).astype(jnp.bfloat16)

    wm = inner_weights(w_state)
    wc = inner_weights(w_cond)
    taps = w_out.reshape(3, 3, fields, hidden)
    variants = jnp.pad(
        tap_variants(taps), ((0, 0), (0, 0), (0, 0), (0, PAD - fields), (0, 0))
    ).reshape(4, 9 * PAD, hidden)[codes]
    wo = jnp.concatenate([guide_weight * variants, (1.0 - guide_weight) * variants], axis=2)
    wo = wo.astype(jnp.bfloat16)
    spread_lanes = (hidden, RIM * width)
    e1 = jnp.broadcast_to(0.5 * embed_first[:, None], spread_lanes)
    e2 = jnp.broadcast_to(0.5 * embed_second[:, None], spread_lanes)
    cuts = [corner_flags(corner_points, tile_row, col_base + p) for p in range(tiles)]
    msk = lane_masks(cuts, side, width)
    icov = inverse_coverage(cuts, side)

    slots = (extent // RIM + 2) // 2
    f32 = jnp.float32
    vmem = pl.BlockSpec(memory_space=pltpu.VMEM)
    updated = pl.pallas_call(
        functools.partial(kernel, side),
        out_shape=jax.ShapeDtypeStruct((side, PAD, width), f32),
        in_specs=[vmem] * 9,
        out_specs=vmem,
        scratch_shapes=[
            pltpu.VMEM((extent, PAD, width), f32),
            pltpu.VMEM((extent, PAD, width), f32),
            pltpu.VMEM((extent, PAD, width), f32),
            pltpu.VMEM((tiles, 3, extent + 2, PAD, width), jnp.bfloat16),
            pltpu.VMEM((tiles, extent // RIM, hidden, RIM * width), f32),
            pltpu.VMEM((tiles, extent + 2, 9 * PAD, width), f32),
            pltpu.VMEM((2, extent, PAD, width), f32),
            pltpu.VMEM((side, PAD, width), f32),
            pltpu.VMEM((3, 2, slots, PAD, width), f32),
            pltpu.VMEM((3, 2, slots, PAD, width), f32),
            pltpu.VMEM((2, 2, RIM, PAD, width), f32),
            pltpu.VMEM((2, 2, slots, PAD, width), f32),
            pltpu.VMEM((2, 2, slots, PAD, width), f32),
            pltpu.SemaphoreType.DMA((5, 8)),
            pltpu.SemaphoreType.DMA((5, 8)),
        ],
        compiler_params=pltpu.CompilerParams(
            collective_id=0, has_side_effects=True, vmem_limit_bytes=50 * 1024 * 1024
        ),
    )(gs, gc, wm, wc, wo, e1, e2, msk, icov)

    updated = jnp.transpose(updated[:, :fields], (1, 0, 2))
    return jnp.concatenate(
        [turned(updated[:, :, p * side : (p + 1) * side], codes[p]) for p in range(tiles)],
        axis=2,
    )


def solution(mesh):
    return jax.shard_map(
        local,
        mesh=mesh,
        in_specs=(
            P("groups", "face", "tile"),
            P("groups", "face", "tile"),
            P(),
            P(),
            P(),
            P(),
            P(),
            P(),
            P(),
        ),
        out_specs=P("groups", "face", "tile"),
        check_vma=False,
    )
```

profile of v0, /device:TPU:1, one launch (start us, length us, event | category | flops | bytes accessed | tf_op | source)
XLA Modules:
  0.0 100.7 jit_solution(16780586480554058990)
XLA Ops:
  0.0 0.8 fusion.37
  0.8 0.6 fusion.41
  2.7 1.3 %fusion.38 = (f32[12,64,64]{2,1,0:T(8,128)S(1)}, f32[12,64,64]{1,2,0:T(8,128)S(1)}, f32[12,64,64]{1,2,0:T(8,128)S(1)}, f32[12,64,64]{2,1,0:T(8,128)S(1)}) fusion(f32[12,64,128]{2,1,0:T(8,128)} %param.10), kind=kLoop, calls=%fused_computation.121 | loop fusion | bytes 1179648 | tf_op jit(solution)/shard_map/slice | solution.py:375
  4.0 0.3 copy.90
  4.3 0.3 copy.92
  4.6 0.5 copy_select_fusion
  6.1 0.7 copy-done.5
  6.8 0.7 fusion.40
  18.2 0.9 fusion.39
  19.5 0.3 copy.88
  19.8 0.7 copy-done.1
  20.5 0.5 copy_select_fusion.2
  21.9 0.7 copy-done.2
  22.7 0.6 gather_fusion.2
  23.3 0.7 copy-done.3
  24.2 0.6 gather_fusion.1
  24.9 0.6 copy-done.4
  25.6 0.6 gather_fusion
  26.3 0.6 copy-done.6
  27.1 0.5 copy-done.7
  27.7 62.4 %shard_map.91 = f32[64,16,128]{2,1,0:T(8,128)S(1)} custom-call(f32[64,16,128]{2,1,0:T(8,128)S(1)} %pad.18.gs, f32[64,16,128]{2,1,0:T(8,128)S(1)} %pad.19.gc, bf16[2,128,144]{2,1,0:T(8,128)(2,1)S(1)} %get-tuple-element.52.wm, bf16[2,128,144]{2,1,0:T(8,128)(2,1)S(1)} %get-tuple-element.51.wc, bf16[2,144,256]{2,1,0:T(8,128)(2,1)S(1)} %pad_maximum_fusion.1.wo, ...), custom_call_target="tpu_custom_call" | custom-call | tf_op jit(solution)/shard_map/pallas_call | solution.py:408
  90.4 0.4 copy.105
  90.8 0.4 copy.106
  99.8 0.9 copy.107
  (78 shorter events, 4.4 us)
Async XLA Ops:
  6.0 12.2 %copy-start = (f32[12,64,128]{2,1,0:T(8,128)S(1)}, f32[12,64,128]{2,1,0:T(8,128)}, u32[]{:S(2)}) copy-start(f32[12,64,128]{2,1,0:T(8,128)} %param.9) | copy-start | bytes 1179652
  6.1 0.7 copy-start.5
  19.5 1.0 copy-start.1
  21.8 0.8 copy-start.2
  23.3 0.8 copy-start.3
  24.7 0.8 copy-start.4
  26.3 0.7 copy-start.6
  27.0 0.7 copy-start.7
where the time goes:
time: 101 us
  Pallas kernels  62.4 us (62%)
  between operations  19.9 us (20%)
  local copies, waits for them, and re-layouts  14.6 us (14%)
  other arithmetic  3.8 us (4%)
    pallas_call x1, Pallas kernels, local(): pl.pallas_call(functools.partial(kernel, side), out_shape=jax.ShapeDtypeS...  62.4 us
    unnamed x16, local copies, waits for them, and re-layouts  4.64 us
    slice x2, local copies, waits for them, and re-layouts, into_rows(): field[:, :, p * side:(p + 1) * side]  2.28 us

commit v1 on v0

--- a/solution.py
+++ b/solution.py
@@ -20,76 +20,20 @@
 scale_second = 1.0 / math.sqrt(1.0 + sigma_second**2)
 
 
-def corner_flags(corner_points, tile_row, tile_col):
-    grid_rows, grid_cols = corner_points.shape
-    next_row = (tile_row + 1) % grid_rows
-    next_col = (tile_col + 1) % grid_cols
-    return (
-        corner_points[tile_row, tile_col],
-        corner_points[tile_row, next_col],
-        corner_points[next_row, tile_col],
-        corner_points[next_row, next_col],
-    )
-
-
-def turned(picture, code):
-    picture = jnp.where(code % 2 == 1, jnp.swapaxes(picture, -1, -2), picture)
-    picture = jnp.where((code == 1) | (code == 2), picture[..., ::-1, :], picture)
-    return jnp.where(code >= 2, picture[..., ::-1], picture)
-
-
-def lane_masks(corner_cuts, side, width):
-    lane = jnp.arange(width, dtype=jnp.int32)
-    masks = []
-    for position, cut in enumerate(corner_cuts):
-        col = (lane - (position * side - RIM)) % width
-        valid = col < side + 2 * RIM
-        left = col < RIM
-        right = valid & (col >= side + RIM)
-        top = valid & ~(left & (cut[0] == 1)) & ~(right & (cut[1] == 1))
-        low = valid & ~(left & (cut[2] == 1)) & ~(right & (cut[3] == 1))
-        masks.append(jnp.stack([top, valid, low]))
-    return jnp.broadcast_to(
-        jnp.stack(masks).astype(jnp.float32)[:, :, None, :], (len(corner_cuts), 3, PAD, width)
-    )
-
-
-def inverse_coverage(corner_cuts, side):
-    local_col = jnp.arange(side, dtype=jnp.int32)
-    left = local_col < RIM
-    right = local_col >= side - RIM
-    rows = []
-    for kind in range(3):
-        parts = []
-        for cut in corner_cuts:
-            cover = 1.0 + left.astype(jnp.float32) + right.astype(jnp.float32)
-            if kind != 1:
-                first, second = (cut[0], cut[1]) if kind == 0 else (cut[2], cut[3])
-                cover = cover + 1.0
-                cover = cover + (left & (first == 0)).astype(jnp.float32)
-                cover = cover + (right & (second == 0)).astype(jnp.float32)
-            parts.append(cover)
-        rows.append(jnp.concatenate(parts))
-    cover = jnp.stack(rows)
-    return jnp.broadcast_to((1.0 / cover)[:, None, :], (3, PAD, cover.shape[1]))
-
-
-def tap_variants(taps):
-    return jnp.stack([jnp.rot90(taps, (4 - quarter) % 4, axes=(0, 1)) for quarter in range(4)])
-
-
 def kernel(
     side,
-    gs, gc, wm, wc, wo, e1, e2, msk, icov,
+    noisy, given, orient, corners, ws_t, wc_t, w_out, e1, e2,
     out,
+    wm, wc, wo, emb, msk, icov, turned_rows, updated,
     exs, exc, exm, win, feat, prod, total, sl1,
     ps, pr, fr, fps, fpr,
     send, recv,
 ):
-    width = gs.shape[2]
+    fields, _, width = noisy.shape
+    hidden = w_out.shape[1]
     extent = side + 2 * RIM
     blocks = extent // RIM
-    tiles = wm.shape[0]
+    tiles = width // side
     n_tile = lax.axis_size("tile")
     n_face = lax.axis_size("face")
     my_tile = lax.axis_index("tile")
@@ -214,12 +158,12 @@
 
         lax.fori_loop(0, tiles * blocks, feature_block, 0)
 
-    def predictions(embedding):
+    def predictions(number):
         def predict_block(step, _):
             p = step // blocks
             block = lax.rem(step, blocks)
             mixed = jnp.dot(wm[p], patch(p, block * RIM), preferred_element_type=jnp.float32)
-            mixed = mixed + embedding[...]
+            mixed = mixed + jnp.concatenate([emb[number]] * RIM, axis=1)
             cond = mixed + feat[p, block]
             plain_hidden = (mixed + mixed * jnp.tanh(mixed)).astype(jnp.bfloat16)
             cond_hidden = (cond + cond * jnp.tanh(cond)).astype(jnp.bfloat16)
@@ -317,10 +261,123 @@
 
         lax.fori_loop(1, blocks - 1, fold_block, 0)
 
-    exc[pl.ds(RIM, side)] = gc[...]
+    codes = [orient[my_face, my_tile * tiles + p] for p in range(tiles)]
+
+    def per_lane(values, shape):
+        return jnp.where(lax.broadcasted_iota(jnp.int32, shape, 1) < side, values[0], values[1])
+
+    def flips_columns(code):
+        return (code == 1) | (code == 2)
+
+    picture_codes = per_lane(codes, (side, width))
+    transposes = lax.rem(picture_codes, 2) == 1
+    source_lane = lax.broadcasted_iota(jnp.int32, (width, width), 0)
+    target_lane = lax.broadcasted_iota(jnp.int32, (width, width), 1)
+    tile_start = jnp.where(target_lane < side, 0, side)
+    mirrored = 2 * tile_start + side - 1 - target_lane
+    wanted = jnp.where(flips_columns(per_lane(codes, (width, width))), mirrored, target_lane)
+    swap = jnp.where(source_lane == wanted, 1.0, 0.0).astype(jnp.bfloat16)
+    swap = jnp.concatenate([swap, swap, swap], axis=0)
+
+    def flipped(value):
+        first = value.astype(jnp.bfloat16)
+        rest = value - first.astype(jnp.float32)
+        second = rest.astype(jnp.bfloat16)
+        third = (rest - second.astype(jnp.float32)).astype(jnp.bfloat16)
+        parts = jnp.concatenate([first, second, third], axis=1)
+        return jnp.dot(parts, swap, preferred_element_type=jnp.float32)
+
+    def transposed(picture):
+        other = jnp.transpose(picture)
+        other = jnp.concatenate([other[:side], other[side:]], axis=1)
+        return jnp.where(transposes, other, picture)
+
+    def source_row(p, row):
+        return jnp.where(codes[p] >= 2, side - 1 - row, row)
+
+    turned_rows[...] = jnp.zeros(turned_rows.shape, jnp.float32)
+
+    def into_rows(field, ex):
+        for channel in range(fields):
+            picture = flipped(transposed(field[channel]))
+            turned_rows[pl.ds(channel, side, stride=PAD)] = picture
+
+        def one_row(row, _):
+            first = turned_rows[pl.ds(PAD * source_row(0, row), PAD)]
+            second = turned_rows[pl.ds(PAD * source_row(1, row), PAD)]
+            ex[row + RIM] = jnp.where(lane < side, first, second)
+            return 0
+
+        lax.fori_loop(0, side, one_row, 0)
+
+    into_rows(given, exc)
     cond_copies = start_exchange(exc, 0, 0)
-    exs[pl.ds(RIM, side)] = gs[...]
+    into_rows(noisy, exs)
     state_copies = start_exchange(exs, 1, 1)
+    grid_rows, grid_cols = corners.shape
+    next_row = lax.rem(my_face + 1, grid_rows)
+    cover_rows = []
+    for p in range(tiles):
+        here = my_tile * tiles + p
+        beside = lax.rem(here + 1, grid_cols)
+        cuts = [
+            corners[my_face, here],
+            corners[my_face, beside],
+            corners[next_row, here],
+            corners[next_row, beside],
+        ]
+        col = lax.rem(lane + width - (p * side - RIM), width)
+        ones = jnp.where(col < extent, 1.0, 0.0)
+        left = col < RIM
+        right = (col >= side + RIM) & (col < extent)
+        cut_low, cut_high = [
+            jnp.where(left, cuts[k], jnp.where(right, cuts[k + 1], 0)) for k in (0, 2)
+        ]
+        msk[p, 0] = jnp.where(cut_low == 1, 0.0, ones)
+        msk[p, 1] = ones
+        msk[p, 2] = jnp.where(cut_high == 1, 0.0, ones)
+        inner = lane - p * side
+        left = inner < RIM
+        right = inner >= side - RIM
+        band = jnp.where(left | right, 1.0, 0.0)
+        cut_low, cut_high = [
+            jnp.where(left, cuts[k], jnp.where(right, cuts[k + 1], 1)) for k in (0, 2)
+        ]
+        cover_rows.append(
+            (
+                2.0 + band + jnp.where(cut_low == 1, 0.0, 1.0),
+                1.0 + band,
+                2.0 + band + jnp.where(cut_high == 1, 0.0, 1.0),
+            )
+        )
+        tap_col = lax.broadcasted_iota(jnp.int32, (9 * PAD, 9 * fields), 0)
+        tap = tap_col // PAD
+        channel = tap_col - tap * PAD
+        a = jnp.where(tap >= 6, 2, jnp.where(tap >= 3, 1, 0))
+        b = tap - 3 * a
+        code = codes[p]
+        source_a = jnp.where(
+            code == 0, a, jnp.where(code == 3, b, jnp.where(code == 2, 2 - a, 2 - b))
+        )
+        source_b = jnp.where(
+            code == 0, b, jnp.where(code == 3, 2 - a, jnp.where(code == 2, 2 - b, a))
+        )
+        source = (3 * source_a + source_b) * fields + channel
+        place = lax.broadcasted_iota(jnp.int32, (9 * PAD, 9 * fields), 1)
+        pick = jnp.where((source == place) & (channel < fields), 1.0, 0.0).astype(jnp.bfloat16)
+        for weights, inner_weights in ((wm, ws_t), (wc, wc_t)):
+            taps = jnp.dot(pick, inner_weights[...], preferred_element_type=jnp.float32)
+            weights[p] = (0.5 * jnp.transpose(taps)).astype(jnp.bfloat16)
+        taps = jnp.dot(pick, w_out[...], preferred_element_type=jnp.float32)
+        wo[p] = jnp.concatenate(
+            [guide_weight * taps, (1.0 - guide_weight) * taps], axis=1
+        ).astype(jnp.bfloat16)
+    for kind in range(3):
+        cover = jnp.where(lane < side, cover_rows[0][kind], cover_rows[1][kind])
+        icov[kind] = 1.0 / cover
+    for number, embedding in enumerate((e1, e2)):
+        spread_out = jnp.broadcast_to(0.5 * embedding[...], (width, hidden))
+        emb[number] = jnp.transpose(spread_out)
     for p in range(tiles):
         prod[p, 0] = jnp.zeros(prod.shape[2:], jnp.float32)
         prod[p, extent + 1] = jnp.zeros(prod.shape[2:], jnp.float32)
@@ -329,26 +386,41 @@
     features()
     finish(state_copies)
     windows(exs, 1, scale_first)
-    predictions(e1)
+    predictions(0)
     copies = start_fold(2, 0)
     finish(copies)
 
     def first_use(row, slope):
         sl1[row - RIM] = slope
-        exm[row] = gs[row - RIM] + step_size * slope
+        exm[row] = exs[row] + step_size * slope
 
     fold(0, first_use)
     copies = start_exchange(exm, 3, 2)
     finish(copies)
     windows(exm, 2, scale_second)
-    predictions(e2)
+    predictions(1)
     copies = start_fold(4, 1)
     finish(copies)
 
     def second_use(row, slope):
-        out[row - RIM] = gs[row - RIM] + 0.5 * step_size * (sl1[row - RIM] + slope)
+        updated[row - RIM] = exs[row] + 0.5 * step_size * (sl1[row - RIM] + slope)
 
     fold(1, second_use)
+
+    def turn_block(block, _):
+        rows = []
+        for k in range(RIM):
+            row = block * RIM + k
+            first = updated[source_row(0, row)]
+            second = updated[source_row(1, row)]
+            rows.append(jnp.where(lane < side, first, second))
+        start = pl.multiple_of(block * RIM * PAD, RIM * PAD)
+        turned_rows[pl.ds(start, RIM * PAD)] = flipped(jnp.concatenate(rows, axis=0))
+        return 0
+
+    lax.fori_loop(0, side // RIM, turn_block, 0)
+    for channel in range(fields):
+        out[channel] = transposed(turned_rows[pl.ds(channel, side, stride=PAD)])
 
 
 def local(
@@ -366,51 +438,24 @@
     tiles = width // side
     extent = side + 2 * RIM
     hidden = w_state.shape[0]
-    tile_row = lax.axis_index("face")
-    col_base = lax.axis_index("tile") * tiles
-    codes = lax.dynamic_slice(orient, (tile_row, col_base), (1, tiles))[0]
-
-    def into_rows(field):
-        parts = [
-            turned(field[:, :, p * side : (p + 1) * side], (4 - codes[p]) % 4)
-            for p in range(tiles)
-        ]
-        whole = jnp.transpose(jnp.concatenate(parts, axis=2), (1, 0, 2))
-        return jnp.pad(whole, ((0, 0), (0, PAD - fields), (0, 0)))
-
-    gs = into_rows(noisy_state)
-    gc = into_rows(conditioning)
-
-    def inner_weights(weights):
-        taps = weights.reshape(hidden, 3, 3, fields).transpose(1, 2, 0, 3)
-        variants = jnp.pad(tap_variants(taps), ((0, 0),) * 4 + ((0, PAD - fields),))
-        variants = variants.transpose(0, 3, 1, 2, 4).reshape(4, hidden, 9 * PAD)
-        return (0.5 * variants[codes]).astype(jnp.bfloat16)
-
-    wm = inner_weights(w_state)
-    wc = inner_weights(w_cond)
-    taps = w_out.reshape(3, 3, fields, hidden)
-    variants = jnp.pad(
-        tap_variants(taps), ((0, 0), (0, 0), (0, 0), (0, PAD - fields), (0, 0))
-    ).reshape(4, 9 * PAD, hidden)[codes]
-    wo = jnp.concatenate([guide_weight * variants, (1.0 - guide_weight) * variants], axis=2)
-    wo = wo.astype(jnp.bfloat16)
-    spread_lanes = (hidden, RIM * width)
-    e1 = jnp.broadcast_to(0.5 * embed_first[:, None], spread_lanes)
-    e2 = jnp.broadcast_to(0.5 * embed_second[:, None], spread_lanes)
-    cuts = [corner_flags(corner_points, tile_row, col_base + p) for p in range(tiles)]
-    msk = lane_masks(cuts, side, width)
-    icov = inverse_coverage(cuts, side)
-
     slots = (extent // RIM + 2) // 2
     f32 = jnp.float32
     vmem = pl.BlockSpec(memory_space=pltpu.VMEM)
-    updated = pl.pallas_call(
+    smem = pl.BlockSpec(memory_space=pltpu.SMEM)
+    return pl.pallas_call(
         functools.partial(kernel, side),
-        out_shape=jax.ShapeDtypeStruct((side, PAD, width), f32),
-        in_specs=[vmem] * 9,
+        out_shape=jax.ShapeDtypeStruct((fields, side, width), f32),
+        in_specs=[vmem, vmem, smem, smem] + [vmem] * 5,
         out_specs=vmem,
         scratch_shapes=[
+            pltpu.VMEM((tiles, hidden, 9 * PAD), jnp.bfloat16),
+            pltpu.VMEM((tiles, hidden, 9 * PAD), jnp.bfloat16),
+            pltpu.VMEM((tiles, 9 * PAD, 2 * hidden), jnp.bfloat16),
+            pltpu.VMEM((2, hidden, width), f32),
+            pltpu.VMEM((tiles, 3, PAD, width), f32),
+            pltpu.VMEM((3, PAD, width), f32),
+            pltpu.VMEM((side * PAD, width), f32),
+            pltpu.VMEM((side, PAD, width), f32),
             pltpu.VMEM((extent, PAD, width), f32),
             pltpu.VMEM((extent, PAD, width), f32),
             pltpu.VMEM((extent, PAD, width), f32),
@@ -430,12 +475,16 @@
         compiler_params=pltpu.CompilerParams(
             collective_id=0, has_side_effects=True, vmem_limit_bytes=50 * 1024 * 1024
         ),
-    )(gs, gc, wm, wc, wo, e1, e2, msk, icov)
-
-    updated = jnp.transpose(updated[:, :fields], (1, 0, 2))
-    return jnp.concatenate(
-        [turned(updated[:, :, p * side : (p + 1) * side], codes[p]) for p in range(tiles)],
-        axis=2,
+    )(
+        noisy_state,
+        conditioning,
+        orient,
+        corner_points,
+        w_state.T,
+        w_cond.T,
+        w_out,
+        embed_first[None],
+        embed_second[None],
     )
 
 

time: 101 us -> 72.5 us (0.72)
  between operations: 19.9 us -> 0.03 us
  local copies, waits for them, and re-layouts: 14.6 us -> 5.67 us
  Pallas kernels: 62.4 us -> 66.4 us
  other arithmetic: 3.8 us -> 0 us
    pallas_call x1, Pallas kernels: 62.4 us -> 66.4 us  [local(): pl.pallas_call(functools.partial(kernel, side), out_shape=jax.ShapeDtypeS...]
    slice x4 -> x0, local copies, waits for them, and re-layouts: 3.24 us -> none  [the longest x2 2.28 us: into_rows(): field[:, :, p * side:(p + 1) * side]]
    select_n x16 -> x0, other arithmetic: 2.61 us -> none  [the longest x3 1.19 us: turned(): picture = jnp.where(code % 2 == 1, jnp.swapaxes(picture, -1, -2), picture)]
    gather x5 -> x0, local copies, waits for them, and re-layouts: 1.92 us -> none  [the longest x4 1.35 us: inner_weights(): return (0.5 * variants[codes]).astype(jnp.bfloat16)]
    transpose x9 -> x0, local copies, waits for them, and re-layouts: 1.73 us -> none  [the longest x6 1.67 us: turned(): picture = jnp.where(code % 2 == 1, jnp.swapaxes(picture, -1, -2), picture)]
    rev x6 -> x0, local copies, waits for them, and re-layouts: 1.14 us -> none  [turned(): return jnp.where(code >= 2, picture[..., ::-1], picture)]
    unnamed x16 -> x19, local copies, waits for them, and re-layouts: 4.64 us -> 5.67 us
where the time goes in v1:
time: 72.5 us; the launch traced here: 72.1 us
  Pallas kernels  66.4 us (92%)
  local copies, waits for them, and re-layouts  5.67 us (8%)
    pallas_call x1, Pallas kernels, local(): pl.pallas_call(functools.partial(kernel, side), out_shape=jax.ShapeDtypeS...  66.4 us
    unnamed x19, local copies, waits for them, and re-layouts  5.67 us

profile of v1, /device:TPU:1, one launch (start us, length us, event | category | flops | bytes accessed | tf_op | source)
XLA Modules:
  0.0 72.1 jit_solution(2804727698214807953)
XLA Ops:
  0.0 0.0 copy-start.6
  0.0 0.0 copy-start.5
  0.0 0.0 copy-start.7
  0.0 0.0 copy-start.8
  0.0 0.7 copy-done.6
  0.7 0.0 copy-done.5
  0.7 0.0 copy-done.7
  0.7 0.0 copy-done.8
  0.7 0.0 copy-start
  0.7 1.0 %copy-done = f32[12,64,128]{2,1,0:T(8,128)S(1)} copy-done((f32[12,64,128]{2,1,0:T(8,128)S(1)}, f32[12,64,128]{2,1,0:T(8,128)}, u32[]{:S(2)}) %copy-start) | copy-done | bytes 393240
  1.7 0.0 copy-start.1
  1.7 1.0 %copy-done.1 = f32[12,64,128]{2,1,0:T(8,128)S(1)} copy-done((f32[12,64,128]{2,1,0:T(8,128)S(1)}, f32[12,64,128]{2,1,0:T(8,128)}, u32[]{:S(2)}) %copy-start.1) | copy-done | bytes 393240
  2.7 0.0 copy-start.2
  2.7 0.7 %copy-done.2 = bf16[128,108]{0,1:T(8,128)(2,1)S(1)} copy-done((bf16[128,108]{0,1:T(8,128)(2,1)S(1)}, bf16[128,108]{0,1:T(8,128)(2,1)}, u32[]{:S(2)}) %copy-start.2) | copy-done | bytes 27672
  3.4 0.0 copy-start.3
  3.4 0.7 %copy-done.3 = bf16[128,108]{0,1:T(8,128)(2,1)S(1)} copy-done((bf16[128,108]{0,1:T(8,128)(2,1)S(1)}, bf16[128,108]{0,1:T(8,128)(2,1)}, u32[]{:S(2)}) %copy-start.3) | copy-done | bytes 27672
  4.2 0.0 copy-start.4
  4.2 0.7 %copy-done.4 = bf16[108,128]{1,0:T(8,128)(2,1)S(1)} copy-done((bf16[108,128]{1,0:T(8,128)(2,1)S(1)}, bf16[108,128]{1,0:T(8,128)(2,1)}, u32[]{:S(2)}) %copy-start.4) | copy-done | bytes 27672
  4.9 66.4 %shard_map.91 = f32[12,64,128]{2,1,0:T(8,128)S(1)} custom-call(f32[12,64,128]{2,1,0:T(8,128)S(1)} %copy-done, f32[12,64,128]{2,1,0:T(8,128)S(1)} %copy-done.1, s32[4,8]{1,0:T(4,128)S(1)} %copy-done.5, s32[4,8]{1,0:T(4,128)S(1)} %copy-done.6, bf16[108,128]{1,0:T(8,128)(2,1)S(1)} %bitcast.4, bf16[108,128]{1,0:T(8,128)(2,1)S(1)} %bitcast.5, ...), custom_call_target="tpu_custom_call" | custom-call | tf_op jit(solution)/shard_map/pallas_call | solution.py:445
  71.4 0.7 %copy.11 = f32[12,64,128]{2,1,0:T(8,128)} copy(f32[12,64,128]{2,1,0:T(8,128)S(1)} %shard_map.91) | data formatting | bytes 786432
Async XLA Ops:
  0.0 0.7 copy-start.6
  0.0 0.7 copy-start.5
  0.0 0.7 copy-start.7
  0.0 0.7 copy-start.8
  0.7 1.0 %copy-start = (f32[12,64,128]{2,1,0:T(8,128)S(1)}, f32[12,64,128]{2,1,0:T(8,128)}, u32[]{:S(2)}) copy-start(f32[12,64,128]{2,1,0:T(8,128)} %noisy.1) | copy-start | bytes 1179652
  1.7 1.0 %copy-start.1 = (f32[12,64,128]{2,1,0:T(8,128)S(1)}, f32[12,64,128]{2,1,0:T(8,128)}, u32[]{:S(2)}) copy-start(f32[12,64,128]{2,1,0:T(8,128)} %given.1) | copy-start | bytes 1179652
  2.7 0.7 %copy-start.2 = (bf16[128,108]{0,1:T(8,128)(2,1)S(1)}, bf16[128,108]{0,1:T(8,128)(2,1)}, u32[]{:S(2)}) copy-start(bf16[128,108]{0,1:T(8,128)(2,1)} %param.13) | copy-start | bytes 82948
  3.4 0.7 %copy-start.3 = (bf16[128,108]{0,1:T(8,128)(2,1)S(1)}, bf16[128,108]{0,1:T(8,128)(2,1)}, u32[]{:S(2)}) copy-start(bf16[128,108]{0,1:T(8,128)(2,1)} %param.14) | copy-start | bytes 82948
  4.2 0.7 %copy-start.4 = (bf16[108,128]{1,0:T(8,128)(2,1)S(1)}, bf16[108,128]{1,0:T(8,128)(2,1)}, u32[]{:S(2)}) copy-start(bf16[108,128]{1,0:T(8,128)(2,1)} %w_out.1) | copy-start | bytes 82948

commit v2 on v1

--- a/solution.py
+++ b/solution.py
@@ -25,7 +25,7 @@
     noisy, given, orient, corners, ws_t, wc_t, w_out, e1, e2,
     out,
     wm, wc, wo, emb, msk, icov, turned_rows, updated,
-    exs, exc, exm, win, feat, prod, total, sl1,
+    exs, exc, exm, win, feat, outs, total, sl1,
     ps, pr, fr, fps, fpr,
     send, recv,
 ):
@@ -68,27 +68,37 @@
         value = jnp.zeros((PAD, width), jnp.float32)
         for k in range(RIM):
             place = k + first
-            moved = pltpu.roll(load(k), lax.rem(shift + RIM * place, width), 1)
+            moved = pltpu.roll(load(k), (shift + RIM * place) % width, 1)
             value = jnp.where(lane // RIM == place, moved, value)
         return value
 
     def unpacked(slot, shift, place):
-        return pltpu.roll(slot, lax.rem(2 * width - shift - RIM * place, width), 1)
+        return pltpu.roll(slot, (-shift - RIM * place) % width, 1)
 
     def kind_of(block, low, high):
         return jnp.where(block == low, 0, jnp.where(block == high, 2, 1))
 
+    def sweep(visit, ends):
+        if ends:
+            visit(0, 0, RIM, 0)
+
+        def pair(slot, _):
+            visit(2 * slot - 1, slot, 0, 1)
+            visit(2 * slot, slot, RIM, 1)
+            return 0
+
+        lax.fori_loop(1, slots - 1, pair, 0)
+        if ends:
+            visit(blocks - 1, slots - 1, 0, 2)
+
     def start_exchange(ex, phase, buf):
-        def pack_block(block, _):
-            slot = (block + 1) // 2
-            first = RIM * lax.rem(block + 1, 2)
+        def pack_block(block, slot, first, _):
             for group in range(2):
                 part = packed(lambda k: ex[block * RIM + k], RIM * group, first)
                 ps[buf, group, slot] = ps[buf, group, slot] + part
-            return 0
 
         ps[buf] = jnp.zeros(ps.shape[1:], jnp.float32)
-        lax.fori_loop(1, blocks - 1, pack_block, 0)
+        sweep(pack_block, False)
         copies = [
             remote(ex.at[pl.ds(RIM, RIM)], ex.at[pl.ds(side + RIM, RIM)], phase, 0, 0, -1),
             remote(ex.at[pl.ds(side, RIM)], ex.at[pl.ds(0, RIM)], phase, 1, 0, 1),
@@ -119,10 +129,7 @@
                 win[p, b, 0] = jnp.zeros((PAD, width), jnp.bfloat16)
                 win[p, b, extent + 1] = jnp.zeros((PAD, width), jnp.bfloat16)
 
-        def window_block(block, _):
-            kind = kind_of(block, 0, blocks - 1)
-            slot = (block + 1) // 2
-            first = RIM * lax.rem(block + 1, 2)
+        def window_block(block, slot, first, kind):
             after = pr[buf, 0, slot]
             before = pr[buf, 1, slot]
             for k in range(RIM):
@@ -135,9 +142,8 @@
                     win[p, 0, row + 1] = pltpu.roll(value, 1, 1).astype(jnp.bfloat16)
                     win[p, 1, row + 1] = value.astype(jnp.bfloat16)
                     win[p, 2, row + 1] = pltpu.roll(value, width - 1, 1).astype(jnp.bfloat16)
-            return 0
-
-        lax.fori_loop(0, blocks, window_block, 0)
+
+        sweep(window_block, True)
 
     def patch(p, first_row):
         taps = []
@@ -159,59 +165,63 @@
         lax.fori_loop(0, tiles * blocks, feature_block, 0)
 
     def predictions(number):
-        def predict_block(step, _):
-            p = step // blocks
-            block = lax.rem(step, blocks)
-            mixed = jnp.dot(wm[p], patch(p, block * RIM), preferred_element_type=jnp.float32)
-            mixed = mixed + jnp.concatenate([emb[number]] * RIM, axis=1)
-            cond = mixed + feat[p, block]
-            plain_hidden = (mixed + mixed * jnp.tanh(mixed)).astype(jnp.bfloat16)
-            cond_hidden = (cond + cond * jnp.tanh(cond)).astype(jnp.bfloat16)
-            both = jnp.concatenate([cond_hidden, plain_hidden], axis=0)
-            z = jnp.dot(wo[p], both, preferred_element_type=jnp.float32)
-            for r in range(RIM):
-                prod[p, block * RIM + 1 + r] = z[:, r * width : (r + 1) * width]
-            return 0
-
-        lax.fori_loop(0, tiles * blocks, predict_block, 0)
+        group = 3 * PAD
+
+        def finish_row(p, place, taps):
+            valid = msk[p, 1]
+            outs[p, place] = (
+                taps[PAD : 2 * PAD]
+                + pltpu.roll(taps[:PAD] * valid, 1, 1)
+                + pltpu.roll(taps[2 * PAD :] * valid, width - 1, 1)
+            )
+
+        def predict_block(block, carry):
+            later = []
+            for p in range(tiles):
+                pending, above = carry[p]
+                mixed = jnp.dot(wm[p], patch(p, block * RIM), preferred_element_type=jnp.float32)
+                mixed = mixed + jnp.concatenate([emb[number]] * RIM, axis=1)
+                cond = mixed + feat[p, block]
+                plain_hidden = (mixed + mixed * jnp.tanh(mixed)).astype(jnp.bfloat16)
+                cond_hidden = (cond + cond * jnp.tanh(cond)).astype(jnp.bfloat16)
+                both = jnp.concatenate([cond_hidden, plain_hidden], axis=0)
+                z = jnp.dot(wo[p], both, preferred_element_type=jnp.float32)
+
+                def part(a, r):
+                    return z[a * group : (a + 1) * group, r * width : (r + 1) * width]
+
+                start = block * RIM
+                finish_row(p, start, pending + part(2, 0))
+                finish_row(p, start + 1, above + part(1, 0) + part(2, 1))
+                for r in range(1, RIM - 1):
+                    finish_row(p, start + 1 + r, part(0, r - 1) + part(1, r) + part(2, r + 1))
+                later.append((part(0, RIM - 2) + part(1, RIM - 1), part(0, RIM - 1)))
+            return tuple(later)
+
+        none = jnp.zeros((group, width), jnp.float32)
+        carry = lax.fori_loop(0, blocks, predict_block, ((none, none),) * tiles)
+        for p in range(tiles):
+            finish_row(p, extent, carry[p][0])
 
     def start_fold(phase, buf):
         fps[buf] = jnp.zeros(fps.shape[1:], jnp.float32)
 
-        def spread_block(block, _):
-            kind = kind_of(block, 0, blocks - 1)
-            slot = (block + 1) // 2
-            first = RIM * lax.rem(block + 1, 2)
+        def spread_block(block, slot, first, kind):
             halves = ([], [])
             for k in range(RIM):
                 row = block * RIM + k
-                outs = []
-                for p in range(tiles):
-                    acc = []
-                    for b in range(3):
-                        acc.append(
-                            prod[p, row, pl.ds(PAD * b, PAD)]
-                            + prod[p, row + 1, pl.ds(PAD * (3 + b), PAD)]
-                            + prod[p, row + 2, pl.ds(PAD * (6 + b), PAD)]
-                        )
-                    valid = msk[p, 1]
-                    summed = (
-                        acc[1]
-                        + pltpu.roll(acc[0] * valid, 1, 1)
-                        + pltpu.roll(acc[2] * valid, width - 1, 1)
-                    )
-                    outs.append(summed * msk[p, kind])
-                total[buf, row] = jnp.where(lane < 3 * width // 4, outs[0], 0.0) + jnp.where(
-                    lane >= width // 4, outs[1], 0.0
+                first_out = outs[0, row + 1] * msk[0, kind]
+                second_out = outs[1, row + 1] * msk[1, kind]
+                total[buf, row] = jnp.where(lane < 3 * width // 4, first_out, 0.0) + jnp.where(
+                    lane >= width // 4, second_out, 0.0
                 )
-                halves[0].append(outs[1])
-                halves[1].append(outs[0])
+                halves[0].append(second_out)
+                halves[1].append(first_out)
             for group in range(2):
                 part = packed(lambda k: halves[group][k], RIM * group, first)
                 fps[buf, group, slot] = fps[buf, group, slot] + part
-            return 0
-
-        lax.fori_loop(0, blocks, spread_block, 0)
+
+        sweep(spread_block, True)
         copies = [
             remote(total.at[buf, pl.ds(0, RIM)], fr.at[buf, 1], phase, 0, 0, -1),
             remote(total.at[buf, pl.ds(side + RIM, RIM)], fr.at[buf, 0], phase, 1, 0, 1),
@@ -242,10 +252,8 @@
         total[buf, pl.ds(RIM, RIM)] = total[buf, pl.ds(RIM, RIM)] + fr[buf, 0]
         total[buf, pl.ds(side, RIM)] = total[buf, pl.ds(side, RIM)] + fr[buf, 1]
 
-        def fold_block(block, _):
+        def fold_block(block, slot, first, _):
             kind = kind_of(block, 1, blocks - 2)
-            slot = (block + 1) // 2
-            first = RIM * lax.rem(block + 1, 2)
             low = fpr[buf, 0, slot]
             high = fpr[buf, 1, slot]
             scale = icov[kind]
@@ -257,9 +265,8 @@
                     lane >= width - RIM, unpacked(high, RIM, first + k), 0.0
                 )
                 use(row, value * scale)
-            return 0
-
-        lax.fori_loop(1, blocks - 1, fold_block, 0)
+
+        sweep(fold_block, False)
 
     codes = [orient[my_face, my_tile * tiles + p] for p in range(tiles)]
 
@@ -378,9 +385,6 @@
     for number, embedding in enumerate((e1, e2)):
         spread_out = jnp.broadcast_to(0.5 * embedding[...], (width, hidden))
         emb[number] = jnp.transpose(spread_out)
-    for p in range(tiles):
-        prod[p, 0] = jnp.zeros(prod.shape[2:], jnp.float32)
-        prod[p, extent + 1] = jnp.zeros(prod.shape[2:], jnp.float32)
     finish(cond_copies)
     windows(exc, 0, 1.0)
     features()
@@ -461,7 +465,7 @@
             pltpu.VMEM((extent, PAD, width), f32),
             pltpu.VMEM((tiles, 3, extent + 2, PAD, width), jnp.bfloat16),
             pltpu.VMEM((tiles, extent // RIM, hidden, RIM * width), f32),
-            pltpu.VMEM((tiles, extent + 2, 9 * PAD, width), f32),
+            pltpu.VMEM((tiles, extent + 1, PAD, width), f32),
             pltpu.VMEM((2, extent, PAD, width), f32),
             pltpu.VMEM((side, PAD, width), f32),
             pltpu.VMEM((3, 2, slots, PAD, width), f32),

time: 72.5 us -> 66.4 us (0.916)
  Pallas kernels: 66.4 us -> 60.3 us
    pallas_call x1, Pallas kernels: 66.4 us -> 60.3 us  [local(): pl.pallas_call(functools.partial(kernel, side), out_shape=jax.ShapeDtypeS...]
where the time goes in v2:
time: 66.4 us; the launch traced here: 66 us
  Pallas kernels  60.3 us (91%)
  local copies, waits for them, and re-layouts  5.67 us (9%)
    pallas_call x1, Pallas kernels, local(): pl.pallas_call(functools.partial(kernel, side), out_shape=jax.ShapeDtypeS...  60.3 us
    unnamed x19, local copies, waits for them, and re-layouts  5.67 us

profile of v2, /device:TPU:1, one launch (start us, length us, event | category | flops | bytes accessed | tf_op | source)
XLA Modules:
  0.0 66.0 jit_solution(4113403593470746904)
XLA Ops:
  0.0 0.0 copy-start.6
  0.0 0.0 copy-start.5
  0.0 0.0 copy-start.7
  0.0 0.0 copy-start.8
  0.0 0.7 %copy-done.6 = s32[4,8]{1,0:T(4,128)S(1)} copy-done((s32[4,8]{1,0:T(4,128)S(1)}, s32[4,8]{1,0:T(4,128)}, u32[]{:S(2)}) %copy-start.6) | copy-done | bytes 152
  0.7 0.0 copy-done.5
  0.7 0.0 copy-done.7
  0.7 0.0 copy-done.8
  0.7 0.0 copy-start
  0.7 1.0 %copy-done = f32[12,64,128]{2,1,0:T(8,128)S(1)} copy-done((f32[12,64,128]{2,1,0:T(8,128)S(1)}, f32[12,64,128]{2,1,0:T(8,128)}, u32[]{:S(2)}) %copy-start) | copy-done | bytes 393240
  1.7 0.0 copy-start.1
  1.7 1.0 %copy-done.1 = f32[12,64,128]{2,1,0:T(8,128)S(1)} copy-done((f32[12,64,128]{2,1,0:T(8,128)S(1)}, f32[12,64,128]{2,1,0:T(8,128)}, u32[]{:S(2)}) %copy-start.1) | copy-done | bytes 393240
  2.7 0.0 copy-start.2
  2.7 0.7 %copy-done.2 = bf16[128,108]{0,1:T(8,128)(2,1)S(1)} copy-done((bf16[128,108]{0,1:T(8,128)(2,1)S(1)}, bf16[128,108]{0,1:T(8,128)(2,1)}, u32[]{:S(2)}) %copy-start.2) | copy-done | bytes 27672
  3.4 0.0 copy-start.3
  3.4 0.7 %copy-done.3 = bf16[128,108]{0,1:T(8,128)(2,1)S(1)} copy-done((bf16[128,108]{0,1:T(8,128)(2,1)S(1)}, bf16[128,108]{0,1:T(8,128)(2,1)}, u32[]{:S(2)}) %copy-start.3) | copy-done | bytes 27672
  4.2 0.0 copy-start.4
  4.2 0.7 %copy-done.4 = bf16[108,128]{1,0:T(8,128)(2,1)S(1)} copy-done((bf16[108,128]{1,0:T(8,128)(2,1)S(1)}, bf16[108,128]{1,0:T(8,128)(2,1)}, u32[]{:S(2)}) %copy-start.4) | copy-done | bytes 27672
  4.9 60.3 %shard_map.91 = f32[12,64,128]{2,1,0:T(8,128)S(1)} custom-call(f32[12,64,128]{2,1,0:T(8,128)S(1)} %copy-done, f32[12,64,128]{2,1,0:T(8,128)S(1)} %copy-done.1, s32[4,8]{1,0:T(4,128)S(1)} %copy-done.5, s32[4,8]{1,0:T(4,128)S(1)} %copy-done.6, bf16[108,128]{1,0:T(8,128)(2,1)S(1)} %bitcast.4, bf16[108,128]{1,0:T(8,128)(2,1)S(1)} %bitcast.5, ...), custom_call_target="tpu_custom_call" | custom-call | tf_op jit(solution)/shard_map/pallas_call | solution.py:449
  65.3 0.7 %copy.11 = f32[12,64,128]{2,1,0:T(8,128)} copy(f32[12,64,128]{2,1,0:T(8,128)S(1)} %shard_map.91) | data formatting | bytes 786432
Async XLA Ops:
  0.0 0.7 %copy-start.6 = (s32[4,8]{1,0:T(4,128)S(1)}, s32[4,8]{1,0:T(4,128)}, u32[]{:S(2)}) copy-start(s32[4,8]{1,0:T(4,128)} %corners.1) | copy-start | bytes 388
  0.0 0.7 %copy-start.5 = (s32[4,8]{1,0:T(4,128)S(1)}, s32[4,8]{1,0:T(4,128)}, u32[]{:S(2)}) copy-start(s32[4,8]{1,0:T(4,128)} %orient.1) | copy-start | bytes 388
  0.0 0.7 %copy-start.7 = (f32[128]{0:T(128)S(1)}, f32[128]{0:T(128)}, u32[]{:S(2)}) copy-start(f32[128]{0:T(128)} %param.16) | copy-start | bytes 1540
  0.0 0.7 %copy-start.8 = (f32[128]{0:T(128)S(1)}, f32[128]{0:T(128)}, u32[]{:S(2)}) copy-start(f32[128]{0:T(128)} %param.17) | copy-start | bytes 1540
  0.7 1.0 %copy-start = (f32[12,64,128]{2,1,0:T(8,128)S(1)}, f32[12,64,128]{2,1,0:T(8,128)}, u32[]{:S(2)}) copy-start(f32[12,64,128]{2,1,0:T(8,128)} %noisy.1) | copy-start | bytes 1179652
  1.7 1.0 %copy-start.1 = (f32[12,64,128]{2,1,0:T(8,128)S(1)}, f32[12,64,128]{2,1,0:T(8,128)}, u32[]{:S(2)}) copy-start(f32[12,64,128]{2,1,0:T(8,128)} %given.1) | copy-start | bytes 1179652
  2.7 0.7 %copy-start.2 = (bf16[128,108]{0,1:T(8,128)(2,1)S(1)}, bf16[128,108]{0,1:T(8,128)(2,1)}, u32[]{:S(2)}) copy-start(bf16[128,108]{0,1:T(8,128)(2,1)} %param.13) | copy-start | bytes 82948
  3.4 0.7 %copy-start.3 = (bf16[128,108]{0,1:T(8,128)(2,1)S(1)}, bf16[128,108]{0,1:T(8,128)(2,1)}, u32[]{:S(2)}) copy-start(bf16[128,108]{0,1:T(8,128)(2,1)} %param.14) | copy-start | bytes 82948
  4.2 0.7 %copy-start.4 = (bf16[108,128]{1,0:T(8,128)(2,1)S(1)}, bf16[108,128]{1,0:T(8,128)(2,1)}, u32[]{:S(2)}) copy-start(bf16[108,128]{1,0:T(8,128)(2,1)} %w_out.1) | copy-start | bytes 82948

commit v3 on v2

--- a/solution.py
+++ b/solution.py
@@ -22,13 +22,28 @@
 
 def kernel(
     side,
-    noisy, given, orient, corners, ws_t, wc_t, w_out, e1, e2,
+    noisy_in, given_in, orient, corners, ws_in, wc_in, w_out_in, e1, e2,
     out,
+    noisy, given, ws_t, wc_t, w_out, fetched,
     wm, wc, wo, emb, msk, icov, turned_rows, updated,
     exs, exc, exm, win, feat, outs, total, sl1,
     ps, pr, fr, fps, fpr,
     send, recv,
 ):
+    fetches = [
+        pltpu.make_async_copy(source, target, fetched.at[number])
+        for number, (source, target) in enumerate(
+            (
+                (given_in, given),
+                (noisy_in, noisy),
+                (ws_in, ws_t),
+                (wc_in, wc_t),
+                (w_out_in, w_out),
+            )
+        )
+    ]
+    for fetch in fetches:
+        fetch.start()
     fields, _, width = noisy.shape
     hidden = w_out.shape[1]
     extent = side + 2 * RIM
@@ -182,9 +197,8 @@
                 mixed = jnp.dot(wm[p], patch(p, block * RIM), preferred_element_type=jnp.float32)
                 mixed = mixed + jnp.concatenate([emb[number]] * RIM, axis=1)
                 cond = mixed + feat[p, block]
-                plain_hidden = (mixed + mixed * jnp.tanh(mixed)).astype(jnp.bfloat16)
-                cond_hidden = (cond + cond * jnp.tanh(cond)).astype(jnp.bfloat16)
-                both = jnp.concatenate([cond_hidden, plain_hidden], axis=0)
+                both = jnp.concatenate([cond, mixed], axis=0).astype(jnp.bfloat16)
+                both = both + both * jnp.tanh(both)
                 z = jnp.dot(wo[p], both, preferred_element_type=jnp.float32)
 
                 def part(a, r):
@@ -305,22 +319,30 @@
     turned_rows[...] = jnp.zeros(turned_rows.shape, jnp.float32)
 
     def into_rows(field, ex):
+        pictures = [transposed(field[channel]) for channel in range(fields)]
+        pictures = flipped(jnp.concatenate(pictures, axis=0))
         for channel in range(fields):
-            picture = flipped(transposed(field[channel]))
+            picture = pictures[channel * side : (channel + 1) * side]
             turned_rows[pl.ds(channel, side, stride=PAD)] = picture
 
-        def one_row(row, _):
-            first = turned_rows[pl.ds(PAD * source_row(0, row), PAD)]
-            second = turned_rows[pl.ds(PAD * source_row(1, row), PAD)]
-            ex[row + RIM] = jnp.where(lane < side, first, second)
+        def some_rows(block, _):
+            for k in range(RIM):
+                row = block * RIM + k
+                first = turned_rows[pl.ds(PAD * source_row(0, row), PAD)]
+                second = turned_rows[pl.ds(PAD * source_row(1, row), PAD)]
+                ex[row + RIM] = jnp.where(lane < side, first, second)
             return 0
 
-        lax.fori_loop(0, side, one_row, 0)
-
+        lax.fori_loop(0, side // RIM, some_rows, 0)
+
+    fetches[0].wait()
     into_rows(given, exc)
     cond_copies = start_exchange(exc, 0, 0)
+    fetches[1].wait()
     into_rows(noisy, exs)
     state_copies = start_exchange(exs, 1, 1)
+    for fetch in fetches[2:]:
+        fetch.wait()
     grid_rows, grid_cols = corners.shape
     next_row = lax.rem(my_face + 1, grid_rows)
     cover_rows = []
@@ -446,12 +468,19 @@
     f32 = jnp.float32
     vmem = pl.BlockSpec(memory_space=pltpu.VMEM)
     smem = pl.BlockSpec(memory_space=pltpu.SMEM)
+    hbm = pl.BlockSpec(memory_space=pltpu.HBM)
     return pl.pallas_call(
         functools.partial(kernel, side),
         out_shape=jax.ShapeDtypeStruct((fields, side, width), f32),
-        in_specs=[vmem, vmem, smem, smem] + [vmem] * 5,
+        in_specs=[hbm, hbm, smem, smem, hbm, hbm, hbm, vmem, vmem],
         out_specs=vmem,
         scratch_shapes=[
+            pltpu.VMEM((fields, side, width), f32),
+            pltpu.VMEM((fields, side, width), f32),
+            pltpu.VMEM((9 * fields, hidden), jnp.bfloat16),
+            pltpu.VMEM((9 * fields, hidden), jnp.bfloat16),
+            pltpu.VMEM((9 * fields, hidden), jnp.bfloat16),
+            pltpu.SemaphoreType.DMA((5,)),
             pltpu.VMEM((tiles, hidden, 9 * PAD), jnp.bfloat16),
             pltpu.VMEM((tiles, hidden, 9 * PAD), jnp.bfloat16),
             pltpu.VMEM((tiles, 9 * PAD, 2 * hidden), jnp.bfloat16),
@@ -477,7 +506,7 @@
             pltpu.SemaphoreType.DMA((5, 8)),
         ],
         compiler_params=pltpu.CompilerParams(
-            collective_id=0, has_side_effects=True, vmem_limit_bytes=50 * 1024 * 1024
+            collective_id=0, has_side_effects=True, vmem_limit_bytes=64 * 1024 * 1024
         ),
     )(
         noisy_state,

time: 66.4 us -> 61.2 us (0.922)
  local copies, waits for them, and re-layouts: 5.67 us -> 1.77 us
  Pallas kernels: 60.3 us -> 59.2 us
    unnamed x19 -> x1, local copies, waits for them, and re-layouts: 5.67 us -> 1.77 us
    pallas_call x1, Pallas kernels: 60.3 us -> 59.2 us  [local(): pl.pallas_call(functools.partial(kernel, side), out_shape=jax.ShapeDtypeS...]
where the time goes in v3:
time: 61.2 us; the launch traced here: 61 us
  Pallas kernels  59.2 us (97%)
  local copies, waits for them, and re-layouts  1.77 us (3%)
    pallas_call x1, Pallas kernels, local(): pl.pallas_call(functools.partial(kernel, side), out_shape=jax.ShapeDtypeS...  59.2 us
    unnamed x1, local copies, waits for them, and re-layouts  1.77 us

profile of v3, /device:TPU:1, one launch (start us, length us, event | category | flops | bytes accessed | tf_op | source)
XLA Modules:
  0.0 61.0 jit_solution(14826846416884157310)
XLA Ops:
  0.0 59.2 %shard_map.91 = f32[12,64,128]{2,1,0:T(8,128)} custom-call(f32[12,64,128]{2,1,0:T(8,128)} %noisy_in.1, f32[12,64,128]{2,1,0:T(8,128)} %given_in.1, s32[4,8]{1,0:T(4,128)} %orient.1, s32[4,8]{1,0:T(4,128)} %corners.1, bf16[108,128]{1,0:T(8,128)(2,1)} %bitcast.4, bf16[108,128]{1,0:T(8,128)(2,1)} %bitcast.5, bf16[108,128]{1,0:T(8,128)(2,1)} %w_out_in.1, ...), custom_call_target="tpu_custom_call" | custom-call | tf_op jit(solution)/shard_map/pallas_call | solution.py:472
  59.2 1.8 %copy.11 = f32[12,64,128]{2,1,0:T(8,128)} copy(f32[12,64,128]{2,1,0:T(8,128)} %shard_map.91) | data formatting | bytes 786432

commit v4 on v3

--- a/solution.py
+++ b/solution.py
@@ -10,6 +10,7 @@
 
 RIM = 8
 PAD = 16
+CHUNK = 2
 MESH = pl.DeviceIdType.MESH
 
 guide_weight = 2.0
@@ -160,12 +161,12 @@
 
         sweep(window_block, True)
 
-    def patch(p, first_row):
+    def patch(p, first_row, count):
         taps = []
         for a in range(3):
             for b in range(3):
-                rows = win[p, b, pl.ds(first_row + a, RIM)]
-                taps.append(jnp.concatenate([rows[r] for r in range(RIM)], axis=1))
+                rows = win[p, b, pl.ds(first_row + a, count)]
+                taps.append(jnp.concatenate([rows[r] for r in range(count)], axis=1))
         return jnp.concatenate(taps, axis=0)
 
     def features():
@@ -173,7 +174,7 @@
             p = step // blocks
             block = lax.rem(step, blocks)
             feat[p, block] = jnp.dot(
-                wc[p], patch(p, block * RIM), preferred_element_type=jnp.float32
+                wc[p], patch(p, block * RIM, RIM), preferred_element_type=jnp.float32
             )
             return 0
 
@@ -191,26 +192,55 @@
             )
 
         def predict_block(block, carry):
-            later = []
-            for p in range(tiles):
+            start = block * RIM
+            chunks = [(p, r) for r in range(0, RIM, CHUNK) for p in range(tiles)]
+            products = {}
+
+            def mix(p, r):
+                value = jnp.dot(
+                    wm[p], patch(p, start + r, CHUNK), preferred_element_type=jnp.float32
+                )
+                return value + jnp.concatenate([emb[number]] * CHUNK, axis=1)
+
+            def hide(p, r, mixed):
+                cond = mixed + feat[p, block, :, pl.ds(r * width, CHUNK * width)]
+                plain_hidden = (mixed + mixed * jnp.tanh(mixed)).astype(jnp.bfloat16)
+                cond_hidden = (cond + cond * jnp.tanh(cond)).astype(jnp.bfloat16)
+                return jnp.concatenate([cond_hidden, plain_hidden], axis=0)
+
+            def project(p, r, both):
+                z = jnp.dot(wo[p], both, preferred_element_type=jnp.float32)
+                for k in range(CHUNK):
+                    products[p, r + k] = z[:, k * width : (k + 1) * width]
+
+            def part(p, a, r):
+                return products[p, r][a * group : (a + 1) * group]
+
+            def finish_rows(p, r):
                 pending, above = carry[p]
-                mixed = jnp.dot(wm[p], patch(p, block * RIM), preferred_element_type=jnp.float32)
-                mixed = mixed + jnp.concatenate([emb[number]] * RIM, axis=1)
-                cond = mixed + feat[p, block]
-                both = jnp.concatenate([cond, mixed], axis=0).astype(jnp.bfloat16)
-                both = both + both * jnp.tanh(both)
-                z = jnp.dot(wo[p], both, preferred_element_type=jnp.float32)
-
-                def part(a, r):
-                    return z[a * group : (a + 1) * group, r * width : (r + 1) * width]
-
-                start = block * RIM
-                finish_row(p, start, pending + part(2, 0))
-                finish_row(p, start + 1, above + part(1, 0) + part(2, 1))
-                for r in range(1, RIM - 1):
-                    finish_row(p, start + 1 + r, part(0, r - 1) + part(1, r) + part(2, r + 1))
-                later.append((part(0, RIM - 2) + part(1, RIM - 1), part(0, RIM - 1)))
-            return tuple(later)
+                for row in range(r, r + CHUNK):
+                    if row == 0:
+                        taps = pending + part(p, 2, 0)
+                    elif row == 1:
+                        taps = above + part(p, 1, 0) + part(p, 2, 1)
+                    else:
+                        taps = part(p, 0, row - 2) + part(p, 1, row - 1) + part(p, 2, row)
+                    finish_row(p, start + row, taps)
+
+            mixes, hiddens = {}, {}
+            for step in range(len(chunks) + 3):
+                if step < len(chunks):
+                    mixes[step] = mix(*chunks[step])
+                if 0 <= step - 2 < len(chunks):
+                    project(*chunks[step - 2], hiddens.pop(step - 2))
+                if 0 <= step - 1 < len(chunks):
+                    hiddens[step - 1] = hide(*chunks[step - 1], mixes.pop(step - 1))
+                if 0 <= step - 3 < len(chunks):
+                    finish_rows(*chunks[step - 3])
+            return tuple(
+                (part(p, 0, RIM - 2) + part(p, 1, RIM - 1), part(p, 0, RIM - 1))
+                for p in range(tiles)
+            )
 
         none = jnp.zeros((group, width), jnp.float32)
         carry = lax.fori_loop(0, blocks, predict_block, ((none, none),) * tiles)

time: 61.2 us -> 60.1 us (0.982)
  Pallas kernels: 59.2 us -> 58.1 us
    pallas_call x1, Pallas kernels: 59.2 us -> 58.1 us  [local(): pl.pallas_call(functools.partial(kernel, side), out_shape=jax.ShapeDtypeS...]
where the time goes in v4:
time: 60.1 us; the launch traced here: 59.9 us
  Pallas kernels  58.1 us (97%)
  local copies, waits for them, and re-layouts  1.77 us (3%)
    pallas_call x1, Pallas kernels, local(): pl.pallas_call(functools.partial(kernel, side), out_shape=jax.ShapeDtypeS...  58.1 us
    unnamed x1, local copies, waits for them, and re-layouts  1.77 us

profile of v4, /device:TPU:1, one launch (start us, length us, event | category | flops | bytes accessed | tf_op | source)
XLA Modules:
  0.0 59.9 jit_solution(12068510042846598447)
XLA Ops:
  0.0 58.1 %shard_map.91 = f32[12,64,128]{2,1,0:T(8,128)} custom-call(f32[12,64,128]{2,1,0:T(8,128)} %noisy_in.1, f32[12,64,128]{2,1,0:T(8,128)} %given_in.1, s32[4,8]{1,0:T(4,128)} %orient.1, s32[4,8]{1,0:T(4,128)} %corners.1, bf16[108,128]{1,0:T(8,128)(2,1)} %bitcast.4, bf16[108,128]{1,0:T(8,128)(2,1)} %bitcast.5, bf16[108,128]{1,0:T(8,128)(2,1)} %w_out_in.1, ...), custom_call_target="tpu_custom_call" | custom-call | tf_op jit(solution)/shard_map/pallas_call | solution.py:502
  58.1 1.8 %copy.11 = f32[12,64,128]{2,1,0:T(8,128)} copy(f32[12,64,128]{2,1,0:T(8,128)} %shard_map.91) | data formatting | bytes 786432

commit v5 on v4

--- a/solution.py
+++ b/solution.py
@@ -19,6 +19,11 @@
 step_size = sigma_second - sigma_first
 scale_first = 1.0 / math.sqrt(1.0 + sigma_first**2)
 scale_second = 1.0 / math.sqrt(1.0 + sigma_second**2)
+
+
+def silu(value):
+    grown = jnp.exp(jnp.minimum(-value, 80.0))
+    return (value * pl.reciprocal(1.0 + grown, approx=True)).astype(jnp.bfloat16)
 
 
 def kernel(
@@ -65,8 +70,6 @@
     barrier = pltpu.get_barrier_semaphore()
     for dt, df in around:
         pl.semaphore_signal(barrier, inc=1, device_id=device(dt, df), device_id_type=MESH)
-    pl.semaphore_wait(barrier, len(around))
-
     lane = lax.broadcasted_iota(jnp.int32, (PAD, width), 1)
     slots = (blocks + 2) // 2
 
@@ -204,9 +207,7 @@
 
             def hide(p, r, mixed):
                 cond = mixed + feat[p, block, :, pl.ds(r * width, CHUNK * width)]
-                plain_hidden = (mixed + mixed * jnp.tanh(mixed)).astype(jnp.bfloat16)
-                cond_hidden = (cond + cond * jnp.tanh(cond)).astype(jnp.bfloat16)
-                return jnp.concatenate([cond_hidden, plain_hidden], axis=0)
+                return jnp.concatenate([silu(cond), silu(mixed)], axis=0)
 
             def project(p, r, both):
                 z = jnp.dot(wo[p], both, preferred_element_type=jnp.float32)
@@ -367,6 +368,7 @@
 
     fetches[0].wait()
     into_rows(given, exc)
+    pl.semaphore_wait(barrier, len(around))
     cond_copies = start_exchange(exc, 0, 0)
     fetches[1].wait()
     into_rows(noisy, exs)
@@ -426,7 +428,7 @@
         pick = jnp.where((source == place) & (channel < fields), 1.0, 0.0).astype(jnp.bfloat16)
         for weights, inner_weights in ((wm, ws_t), (wc, wc_t)):
             taps = jnp.dot(pick, inner_weights[...], preferred_element_type=jnp.float32)
-            weights[p] = (0.5 * jnp.transpose(taps)).astype(jnp.bfloat16)
+            weights[p] = jnp.transpose(taps).astype(jnp.bfloat16)
         taps = jnp.dot(pick, w_out[...], preferred_element_type=jnp.float32)
         wo[p] = jnp.concatenate(
             [guide_weight * taps, (1.0 - guide_weight) * taps], axis=1
@@ -435,7 +437,7 @@
         cover = jnp.where(lane < side, cover_rows[0][kind], cover_rows[1][kind])
         icov[kind] = 1.0 / cover
     for number, embedding in enumerate((e1, e2)):
-        spread_out = jnp.broadcast_to(0.5 * embedding[...], (width, hidden))
+        spread_out = jnp.broadcast_to(embedding[...], (width, hidden))
         emb[number] = jnp.transpose(spread_out)
     finish(cond_copies)
     windows(exc, 0, 1.0)

time: 60.1 us -> 64.2 us (1.068)
  Pallas kernels: 58.1 us -> 62.1 us
    pallas_call x1, Pallas kernels: 58.1 us -> 62.1 us  [local(): pl.pallas_call(functools.partial(kernel, side), out_shape=jax.ShapeDtypeS...]
where the time goes in v5:
time: 64.2 us; the launch traced here: 63.8 us
  Pallas kernels  62.1 us (97%)
  local copies, waits for them, and re-layouts  1.77 us (3%)
    pallas_call x1, Pallas kernels, local(): pl.pallas_call(functools.partial(kernel, side), out_shape=jax.ShapeDtypeS...  62.1 us
    unnamed x1, local copies, waits for them, and re-layouts  1.77 us

profile of v5, /device:TPU:1, one launch (start us, length us, event | category | flops | bytes accessed | tf_op | source)
XLA Modules:
  0.0 63.8 jit_solution(2027940672346568221)
XLA Ops:
  0.0 62.1 %shard_map.91 = f32[12,64,128]{2,1,0:T(8,128)} custom-call(f32[12,64,128]{2,1,0:T(8,128)} %noisy_in.1, f32[12,64,128]{2,1,0:T(8,128)} %given_in.1, s32[4,8]{1,0:T(4,128)} %orient.1, s32[4,8]{1,0:T(4,128)} %corners.1, bf16[108,128]{1,0:T(8,128)(2,1)} %bitcast.4, bf16[108,128]{1,0:T(8,128)(2,1)} %bitcast.5, bf16[108,128]{1,0:T(8,128)(2,1)} %w_out_in.1, ...), custom_call_target="tpu_custom_call" | custom-call | tf_op jit(solution)/shard_map/pallas_call | solution.py:504
  62.1 1.8 %copy.11 = f32[12,64,128]{2,1,0:T(8,128)} copy(f32[12,64,128]{2,1,0:T(8,128)} %shard_map.91) | data formatting | bytes 786432

commit v6 on v5

--- a/solution.py
+++ b/solution.py
@@ -22,8 +22,7 @@
 
 
 def silu(value):
-    grown = jnp.exp(jnp.minimum(-value, 80.0))
-    return (value * pl.reciprocal(1.0 + grown, approx=True)).astype(jnp.bfloat16)
+    return (value + value * jnp.tanh(value)).astype(jnp.bfloat16)
 
 
 def kernel(
@@ -88,7 +87,8 @@
         for k in range(RIM):
             place = k + first
             moved = pltpu.roll(load(k), (shift + RIM * place) % width, 1)
-            value = jnp.where(lane // RIM == place, moved, value)
+            inside = (lane >= RIM * place) & (lane < RIM * (place + 1))
+            value = jnp.where(inside, moved, value)
         return value
 
     def unpacked(slot, shift, place):
@@ -173,15 +173,14 @@
         return jnp.concatenate(taps, axis=0)
 
     def features():
-        def feature_block(step, _):
-            p = step // blocks
-            block = lax.rem(step, blocks)
-            feat[p, block] = jnp.dot(
-                wc[p], patch(p, block * RIM, RIM), preferred_element_type=jnp.float32
-            )
+        def feature_block(block, _):
+            for p in range(tiles):
+                feat[p, block] = jnp.dot(
+                    wc[p], patch(p, block * RIM, RIM), preferred_element_type=jnp.float32
+                )
             return 0
 
-        lax.fori_loop(0, tiles * blocks, feature_block, 0)
+        lax.fori_loop(0, blocks, feature_block, 0)
 
     def predictions(number):
         group = 3 * PAD
@@ -322,7 +321,7 @@
         return (code == 1) | (code == 2)
 
     picture_codes = per_lane(codes, (side, width))
-    transposes = lax.rem(picture_codes, 2) == 1
+    transposes = (picture_codes == 1) | (picture_codes == 3)
     source_lane = lax.broadcasted_iota(jnp.int32, (width, width), 0)
     target_lane = lax.broadcasted_iota(jnp.int32, (width, width), 1)
     tile_start = jnp.where(target_lane < side, 0, side)
@@ -387,7 +386,8 @@
             corners[next_row, here],
             corners[next_row, beside],
         ]
-        col = lax.rem(lane + width - (p * side - RIM), width)
+        col = lane - (p * side - RIM)
+        col = jnp.where(col < 0, col + width, jnp.where(col >= width, col - width, col))
         ones = jnp.where(col < extent, 1.0, 0.0)
         left = col < RIM
         right = (col >= side + RIM) & (col < extent)
@@ -412,7 +412,7 @@
             )
         )
         tap_col = lax.broadcasted_iota(jnp.int32, (9 * PAD, 9 * fields), 0)
-        tap = tap_col // PAD
+        tap = sum(jnp.where(tap_col >= PAD * k, 1, 0) for k in range(1, 9))
         channel = tap_col - tap * PAD
         a = jnp.where(tap >= 6, 2, jnp.where(tap >= 3, 1, 0))
         b = tap - 3 * a
@@ -428,7 +428,7 @@
         pick = jnp.where((source == place) & (channel < fields), 1.0, 0.0).astype(jnp.bfloat16)
         for weights, inner_weights in ((wm, ws_t), (wc, wc_t)):
             taps = jnp.dot(pick, inner_weights[...], preferred_element_type=jnp.float32)
-            weights[p] = jnp.transpose(taps).astype(jnp.bfloat16)
+            weights[p] = (0.5 * jnp.transpose(taps)).astype(jnp.bfloat16)
         taps = jnp.dot(pick, w_out[...], preferred_element_type=jnp.float32)
         wo[p] = jnp.concatenate(
             [guide_weight * taps, (1.0 - guide_weight) * taps], axis=1
@@ -437,7 +437,7 @@
         cover = jnp.where(lane < side, cover_rows[0][kind], cover_rows[1][kind])
         icov[kind] = 1.0 / cover
     for number, embedding in enumerate((e1, e2)):
-        spread_out = jnp.broadcast_to(embedding[...], (width, hidden))
+        spread_out = jnp.broadcast_to(0.5 * embedding[...], (width, hidden))
         emb[number] = jnp.transpose(spread_out)
     finish(cond_copies)
     windows(exc, 0, 1.0)

time: 64.2 us -> 58.3 us (0.908)
  Pallas kernels: 62.1 us -> 56.2 us
    pallas_call x1, Pallas kernels: 62.1 us -> 56.2 us  [local(): pl.pallas_call(functools.partial(kernel, side), out_shape=jax.ShapeDtypeS...]
where the time goes in v6:
time: 58.3 us; the launch traced here: 58 us
  Pallas kernels  56.2 us (96%)
  local copies, waits for them, and re-layouts  1.77 us (3%)
    pallas_call x1, Pallas kernels, local(): pl.pallas_call(functools.partial(kernel, side), out_shape=jax.ShapeDtypeS...  56.2 us
    unnamed x1, local copies, waits for them, and re-layouts  1.77 us

profile of v6, /device:TPU:1, one launch (start us, length us, event | category | flops | bytes accessed | tf_op | source)
XLA Modules:
  0.0 58.0 jit_solution(18353198757329067773)
XLA Ops:
  0.0 56.2 %shard_map.91 = f32[12,64,128]{2,1,0:T(8,128)} custom-call(f32[12,64,128]{2,1,0:T(8,128)} %noisy_in.1, f32[12,64,128]{2,1,0:T(8,128)} %given_in.1, s32[4,8]{1,0:T(4,128)} %orient.1, s32[4,8]{1,0:T(4,128)} %corners.1, bf16[108,128]{1,0:T(8,128)(2,1)} %bitcast.4, bf16[108,128]{1,0:T(8,128)(2,1)} %bitcast.5, bf16[108,128]{1,0:T(8,128)(2,1)} %w_out_in.1, ...), custom_call_target="tpu_custom_call" | custom-call | tf_op jit(solution)/shard_map/pallas_call | solution.py:504
  56.2 1.8 %copy.11 = f32[12,64,128]{2,1,0:T(8,128)} copy(f32[12,64,128]{2,1,0:T(8,128)} %shard_map.91) | data formatting | bytes 786432

commit v7 on v6

--- a/solution.py
+++ b/solution.py
@@ -10,7 +10,7 @@
 
 RIM = 8
 PAD = 16
-CHUNK = 2
+CHUNK = 4
 MESH = pl.DeviceIdType.MESH
 
 guide_weight = 2.0

time: 58.3 us -> 58.7 us (level)
  no operation moved by 1% of the time
where the time goes in v7:
time: 58.7 us; the launch traced here: 58.4 us
  Pallas kernels  56.6 us (96%)
  local copies, waits for them, and re-layouts  1.77 us (3%)
    pallas_call x1, Pallas kernels, local(): pl.pallas_call(functools.partial(kernel, side), out_shape=jax.ShapeDtypeS...  56.6 us
    unnamed x1, local copies, waits for them, and re-layouts  1.77 us

profile of v7, /device:TPU:1, one launch (start us, length us, event | category | flops | bytes accessed | tf_op | source)
XLA Modules:
  0.0 58.4 jit_solution(6044352973933516386)
XLA Ops:
  0.0 56.6 %shard_map.91 = f32[12,64,128]{2,1,0:T(8,128)} custom-call(f32[12,64,128]{2,1,0:T(8,128)} %noisy_in.1, f32[12,64,128]{2,1,0:T(8,128)} %given_in.1, s32[4,8]{1,0:T(4,128)} %orient.1, s32[4,8]{1,0:T(4,128)} %corners.1, bf16[108,128]{1,0:T(8,128)(2,1)} %bitcast.4, bf16[108,128]{1,0:T(8,128)(2,1)} %bitcast.5, bf16[108,128]{1,0:T(8,128)(2,1)} %w_out_in.1, ...), custom_call_target="tpu_custom_call" | custom-call | tf_op jit(solution)/shard_map/pallas_call | solution.py:504
  56.6 1.8 %copy.11 = f32[12,64,128]{2,1,0:T(8,128)} copy(f32[12,64,128]{2,1,0:T(8,128)} %shard_map.91) | data formatting | bytes 786432
